TPU v7x, 32 devices: a whole 2x2x4 slice. The times are simulated.
32 devices in a mesh: grp: 2 (over y), row: 16 (over z, x, core).
Axes of the slice: x: 2, y: 2, z: 4, core: 2. Of those that a mesh axis runs over, the one named last changes fastest.
Arguments:
- features: bfloat16 [16384, 256], P(('grp', 'row')), may hold values from -6 to 6
- weight: bfloat16 [256, 256], replicated, may hold values from -0.375 to 0.375
- block_vals: bfloat16 [2, 128, 16, 128, 128], P('grp', 'row'), may hold values from -0.125 to 0.125
- block_cols: int32 [2, 128, 16], P('grp', 'row'), may hold values from 0 to 63, as said below
- block_count: int32 [2, 128], P('grp', 'row'), may hold values from 1 to 16, as said below
- cotangent: bfloat16 [16384, 256], P(('grp', 'row')), may hold values from -6 to 6
Outputs:
- activated: bfloat16 [16384, 256], P(('grp', 'row'))
- weight_grad: float32 [256, 256], replicated
- input_grad: bfloat16 [16384, 256], P(('grp', 'row'))
Inputs may be any that keep to these rules, and one draw needn't show every extreme that they name: `block_cols`: within one destination row block the 16 column blocks are distinct and ascending. `block_count`: in every draw some device holds 16 live slots in each of its row blocks.
All inputs are finite; a program needn't handle non-finite values.
Results may differ from a plain program's by a relative error of at most 0.0062.
Values may be sent and summed in bfloat16 or wider, within the bound.
A program may use at most 128 MiB of HBM per device.

v0:
```python
import math

import jax
import jax.numpy as jnp
from jax import lax
from jax.sharding import PartitionSpec as P


def silu_slope(pre):
    sigma = jax.nn.sigmoid(pre)
    return sigma * (1.0 + pre * (1.0 - sigma))


def body(features, weight, block_vals, block_cols, block_count, cotangent):
    rows_dev, width = features.shape
    block = block_vals.shape[-1]
    slot_total = block_vals.shape[2]
    groups = lax.axis_size("grp")
    members = lax.axis_size("row")
    verts = rows_dev * groups * members
    slots = jnp.arange(slot_total)
    gathered = lax.all_gather(features, "row", axis=0, tiled=True)
    col_blocks = gathered.shape[0] // block
    panel_blocks = gathered.reshape(col_blocks, block, width)

    def aggregate(items):
        values, columns, count = items
        masked = jnp.where((slots < count)[:, None, None], values, jnp.zeros_like(values))
        picked = panel_blocks[columns]
        return jnp.einsum("kij,kjf->if", masked, picked, preferred_element_type=jnp.float32)

    partial_value = lax.map(aggregate, (block_vals[0], block_cols[0], block_count[0])).reshape(
        -1, width
    )
    summed = lax.psum(partial_value, "grp")
    aggregated = summed.astype(jnp.bfloat16)
    cot_rows = lax.all_gather(cotangent, "grp", axis=0, tiled=True)
    pre = jnp.dot(aggregated, weight, preferred_element_type=jnp.float32)
    pre_grad = (cot_rows.astype(jnp.float32) * silu_slope(pre)).astype(jnp.bfloat16)
    offset = lax.axis_index("grp") * rows_dev
    activated = lax.dynamic_slice_in_dim(jax.nn.silu(pre), offset, rows_dev, 0).astype(jnp.bfloat16)
    mine_agg = lax.dynamic_slice_in_dim(aggregated, offset, rows_dev, 0)
    mine_grad = lax.dynamic_slice_in_dim(pre_grad, offset, rows_dev, 0)
    local_grad = jnp.dot(mine_agg.T, mine_grad, preferred_element_type=jnp.float32)
    rows_grad = jnp.dot(pre_grad, weight.T, preferred_element_type=jnp.float32).astype(jnp.bfloat16)
    weight_grad = lax.psum(local_grad, ("grp", "row")) * (1.0 / math.sqrt(verts))
    by_block = rows_grad.reshape(-1, block, width)

    def spread(carry, items):
        values, columns, count, grad_block = items
        masked = jnp.where((slots < count)[:, None, None], values, jnp.zeros_like(values))
        contrib = jnp.einsum("kij,if->kjf", masked, grad_block, preferred_element_type=jnp.float32)
        return (carry.at[columns].add(contrib), None)

    total, unused = lax.scan(
        spread,
        jnp.zeros((col_blocks, block, width), jnp.float32),
        (block_vals[0], block_cols[0], block_count[0], by_block),
    )
    term = total.reshape(-1, width)
    input_grad = lax.psum_scatter(term, "row", scatter_dimension=0, tiled=True).astype(jnp.bfloat16)
    return (activated, weight_grad, input_grad)


def solution(mesh):
    placed = (
        P(("grp", "row"), None),
        P(),
        P("grp", "row", None, None, None),
        P("grp", "row", None),
        P("grp", "row"),
        P(("grp", "row"), None),
    )
    return jax.shard_map(
        body,
        mesh=mesh,
        in_specs=placed,
        out_specs=(P(("grp", "row"), None), P(), P(("grp", "row"), None)),
        check_vma=False,
    )
```

profile of v0, /device:TPU:0, one launch (start us, length us, event | category | flops | bytes accessed | tf_op | source)
XLA Modules:
  0.0 384.9 jit_solution(17862340102701671453)
XLA Ops:
  8.0 6.5 %copy.9 = bf16[1,8,16,128,128]{3,4,2,1,0:T(8,128)(2,1)} copy(bf16[1,8,16,128,128]{4,3,2,1,0:T(8,128)(2,1)} %param.12) | data formatting | bytes 8388608 | tf_op args[2]
  14.6 9.9 %all_gather.7 = bf16[1024,256]{1,0:T(8,128)(2,1)S(1)} all-gather(bf16[512,256]{1,0:T(8,128)(2,1)S(1)} %copy-done.3), channel_id=1, replica_groups=mesh['grp'=2,'row'=16] {'grp'}, dimensions={0}, use_global_device_ids=true | all-gather | bytes 786432 | tf_op jit(solution)/shard_map/all_gather | solution.py:37
  24.5 39.0 %all-gather.2.cloned.1.call-done = bf16[8192,256]{1,0:T(8,128)(2,1)} async-done(((bf16[512,256]{1,0:T(8,128)(2,1)}), bf16[8192,256]{1,0:T(8,128)(2,1)}) %all-gather.2.cloned.1.call-update) | async-done | bytes 4194320 | tf_op jit(solution)/shard_map/all_gather | solution.py:22
  63.5 49.4 %while.22 = (s32[]{:T(128)}, f32[8,128,256]{2,1,0:T(8,128)S(1)}, s32[8]{0:T(128)S(1)}, bf16[8,16,128,128]{3,2,1,0:T(8,128)(2,1)}, s32[8,16]{1,0:T(8,128)}, /*index=5*/bf16[64,128,256]{2,1,0:T(8,128)(2,1)}, s32[]{:T(128)}) while((s32[]{:T(128)}, f32[8,128,256]{2,1,0:T(8,128)S(1)}, s32[8]{0:T(128)S(1)}, ...), condition=%wide.region_1.2_spmd.clone, body=%wide.region_0.1_spmd.clone.sunk | while | flops 134480960 | bytes 3807097 | solution.py:32
  65.4 2.8 gather_fusion
  71.6 2.8 gather_fusion
  77.8 2.8 gather_fusion
  84.0 2.8 gather_fusion
  90.1 2.8 gather_fusion
  96.3 2.8 gather_fusion
  102.5 2.8 gather_fusion
  112.9 29.9 %all-reduce.4 = bf16[1024,256]{1,0:T(8,128)(2,1)S(1)} all-reduce(f32[1024,256]{1,0:T(8,128)S(1)} %bitcast.73), channel_id=1, replica_groups=mesh['grp'=2,'row'=16] {'grp'}, use_global_device_ids=true, to_apply=%region_2.3 | all-reduce | flops 262144 | bytes 1572864 | tf_op jit(solution)/shard_map/psum | solution.py:35
  146.1 4.3 %broadcast_in_dim.28 = f32[64,128,256]{2,1,0:T(8,128)} broadcast(f32[]{:T(128)} %constant.29.clone.1), dimensions={} | broadcast | bytes 8388612 | tf_op jit(solution)/shard_map/broadcast_in_dim | solution.py:57
  150.3 64.6 %while.23 = (s32[]{:T(128)}, f32[64,128,256]{2,1,0:T(8,128)}, s32[8,16]{1,0:T(8,128)}, s32[8]{0:T(128)S(1)}, bf16[8,16,128,128]{2,3,1,0:T(8,128)(2,1)}, /*index=5*/bf16[8,128,256]{2,1,0:T(8,128)(2,1)S(1)}, s32[]{:T(128)}) while((s32[]{:T(128)}, f32[64,128,256]{2,1,0:T(8,128)}, s32[8,16]{1,0:T(8,128)}, s32[8]{0:T(128)S(1)}, ...), condition=%wide.region_6.7_spmd.clone, body=%wide.region_4.6_spmd.clone.sunk | while | flops 135004224 | bytes 8980281 | solution.py:55
  153.8 4.6 %scatter_fusion = f32[64,128,256]{2,1,0:T(8,128)} fusion(f32[64,128,256]{2,1,0:T(8,128)} %get-tuple-element.243, s32[16]{0:T(128)S(1)} %fusion.46, f32[16,128,256]{2,1,0:T(8,128)S(1)} %fusion.47), kind=kCustom, calls=%fused_computation.1.clone.clone.1 | custom fusion | flops 524288 | bytes 6291520 | tf_op jit(solution)/shard_map/while/body/eval_jaxpr/scatter-add | solution.py:53
  161.9 4.6 %scatter_fusion = f32[64,128,256]{2,1,0:T(8,128)} fusion(f32[64,128,256]{2,1,0:T(8,128)} %get-tuple-element.243, s32[16]{0:T(128)S(1)} %fusion.46, f32[16,128,256]{2,1,0:T(8,128)S(1)} %fusion.47), kind=kCustom, calls=%fused_computation.1.clone.clone.1 | custom fusion | flops 524288 | bytes 6291520 | tf_op jit(solution)/shard_map/while/body/eval_jaxpr/scatter-add | solution.py:53
  169.9 4.6 %scatter_fusion = f32[64,128,256]{2,1,0:T(8,128)} fusion(f32[64,128,256]{2,1,0:T(8,128)} %get-tuple-element.243, s32[16]{0:T(128)S(1)} %fusion.46, f32[16,128,256]{2,1,0:T(8,128)S(1)} %fusion.47), kind=kCustom, calls=%fused_computation.1.clone.clone.1 | custom fusion | flops 524288 | bytes 6291520 | tf_op jit(solution)/shard_map/while/body/eval_jaxpr/scatter-add | solution.py:53
  178.0 4.6 %scatter_fusion = f32[64,128,256]{2,1,0:T(8,128)} fusion(f32[64,128,256]{2,1,0:T(8,128)} %get-tuple-element.243, s32[16]{0:T(128)S(1)} %fusion.46, f32[16,128,256]{2,1,0:T(8,128)S(1)} %fusion.47), kind=kCustom, calls=%fused_computation.1.clone.clone.1 | custom fusion | flops 524288 | bytes 6291520 | tf_op jit(solution)/shard_map/while/body/eval_jaxpr/scatter-add | solution.py:53
  186.1 4.6 %scatter_fusion = f32[64,128,256]{2,1,0:T(8,128)} fusion(f32[64,128,256]{2,1,0:T(8,128)} %get-tuple-element.243, s32[16]{0:T(128)S(1)} %fusion.46, f32[16,128,256]{2,1,0:T(8,128)S(1)} %fusion.47), kind=kCustom, calls=%fused_computation.1.clone.clone.1 | custom fusion | flops 524288 | bytes 6291520 | tf_op jit(solution)/shard_map/while/body/eval_jaxpr/scatter-add | solution.py:53
  194.1 4.6 %scatter_fusion = f32[64,128,256]{2,1,0:T(8,128)} fusion(f32[64,128,256]{2,1,0:T(8,128)} %get-tuple-element.243, s32[16]{0:T(128)S(1)} %fusion.46, f32[16,128,256]{2,1,0:T(8,128)S(1)} %fusion.47), kind=kCustom, calls=%fused_computation.1.clone.clone.1 | custom fusion | flops 524288 | bytes 6291520 | tf_op jit(solution)/shard_map/while/body/eval_jaxpr/scatter-add | solution.py:53
  202.2 4.7 %scatter_fusion = f32[64,128,256]{2,1,0:T(8,128)} fusion(f32[64,128,256]{2,1,0:T(8,128)} %get-tuple-element.243, s32[16]{0:T(128)S(1)} %fusion.46, f32[16,128,256]{2,1,0:T(8,128)S(1)} %fusion.47), kind=kCustom, calls=%fused_computation.1.clone.clone.1 | custom fusion | flops 524288 | bytes 6291520 | tf_op jit(solution)/shard_map/while/body/eval_jaxpr/scatter-add | solution.py:53
  210.3 4.6 %scatter_fusion = f32[64,128,256]{2,1,0:T(8,128)} fusion(f32[64,128,256]{2,1,0:T(8,128)} %get-tuple-element.243, s32[16]{0:T(128)S(1)} %fusion.46, f32[16,128,256]{2,1,0:T(8,128)S(1)} %fusion.47), kind=kCustom, calls=%fused_computation.1.clone.clone.1 | custom fusion | flops 524288 | bytes 6291520 | tf_op jit(solution)/shard_map/while/body/eval_jaxpr/scatter-add | solution.py:53
  217.2 51.6 %all-reduce.3.cloned.1.call-done = f32[256,256]{1,0:T(8,128)} async-done(((f32[256,256]{1,0:T(8,128)}), f32[256,256]{1,0:T(8,128)}) %all-reduce.3.cloned.1.call-update) | async-done | bytes 262160 | tf_op jit(solution)/shard_map/psum | solution.py:46
  270.5 106.1 %reduce-scatter.2.cloned.1.call-done = f32[512,256]{1,0:T(8,128)} async-done(((f32[8192,256]{1,0:T(8,128)}), f32[512,256]{1,0:T(8,128)}) %reduce-scatter.2.cloned.1.call-update) | async-done | bytes 524304 | tf_op jit(solution)/shard_map/reduce_scatter | solution.py:61
  (96 shorter events, 66.8 us)
Async XLA Ops:
  7.2 135.7 %copy-start = (bf16[256,256]{1,0:T(8,128)(2,1)S(1)}, bf16[256,256]{1,0:T(8,128)(2,1)}, u32[]{:S(2)}) copy-start(bf16[256,256]{1,0:T(8,128)(2,1)} %param.11) | copy-start | bytes 393220
  7.2 56.3 %all-gather.2.cloned.1.call-start = ((), (), s32[]{:S(2)}) async-start(), calls=%async_computation.1 | async-start | bytes 4456448 | tf_op jit(solution)/shard_map/all_gather | solution.py:22
  7.9 260.9 %all-reduce.3.cloned.1.call-start = ((), (), s32[]{:S(2)}) async-start(), calls=%async_computation.2 | async-start | bytes 524288 | tf_op jit(solution)/shard_map/psum | solution.py:46
  8.0 6.6 %copy-start.3 = (bf16[512,256]{1,0:T(8,128)(2,1)S(1)}, bf16[512,256]{1,0:T(8,128)(2,1)}, u32[]{:S(2)}) copy-start(bf16[512,256]{1,0:T(8,128)(2,1)} %param.15) | copy-start | bytes 786436
  8.0 55.5 %copy-start.4 = (s32[1,8]{1,0:T(1,128)S(1)}, s32[1,8]{1,0:T(1,128)}, u32[]{:S(2)}) copy-start(s32[1,8]{1,0:T(1,128)} %param.14) | copy-start | bytes 100
  146.0 230.5 %reduce-scatter.2.cloned.1.call-start = ((), (), s32[]{:S(2)}) async-start(), calls=%async_computation.3 | async-start | bytes 8912896 | tf_op jit(solution)/shard_map/reduce_scatter | solution.py:61
  214.9 1.2 copy-start.1
  214.9 1.5 copy-start.2
Sparse Core Ops, SparseCore 0:
  10.2 53.2 all-gather.1
  146.1 122.6 all-reduce.2
  272.9 103.6 reduce-scatter.1
where the time goes:
time: 387 us; the launch traced here: 385 us
  waiting for transfers between devices  197 us (51%)
  other arithmetic  62.7 us (16%)
  local copies, waits for them, and re-layouts  44.1 us (11%)
  blocking collectives  39.9 us (10%)
  matrix products  26.5 us (7%)
  between operations  13.8 us (4%)
    reduce_scatter x1, waiting for transfers between devices, body(): lax.psum_scatter(term, 'row', scatter_dimension=0, tiled=True)  106 us
    psum x1, waiting for transfers between devices, body(): lax.psum(local_grad, ('grp', 'row')) * (1.0 / math.sqrt(verts))  51.6 us
    all_gather x1, waiting for transfers between devices, body(): gathered = lax.all_gather(features, 'row', axis=0, tiled=True)  39 us
    scatter-add x8, other arithmetic, spread(): return (carry.at[columns].add(contrib), None)  36.9 us
    psum x1, blocking collectives, body(): summed = lax.psum(partial_value, 'grp')  29.9 us
    gather x8, local copies, waits for them, and re-layouts, aggregate(): picked = panel_blocks[columns]  22.4 us
    dot_general x8, matrix products, spread(): jnp.einsum('kij,if->kjf', masked, grad_block, preferred_element_type=jnp....  12.1 us
    dot_general x8, matrix products, aggregate(): jnp.einsum('kij,kjf->if', masked, picked, preferred_element_type=jnp.floa...  11.2 us
  transfers between devices with their start and end apart: 3, of which 3 were waited for; matrix products, arithmetic and copies ran while one was open for 20% of the time, Pallas kernels for 0%

commit v1 on v0

v1 whole, which is shorter than its diff:
```python
import functools
import math

import jax
import jax.numpy as jnp
from jax import lax
from jax.experimental import pallas as pl
from jax.experimental.pallas import tpu as pltpu
from jax.sharding import PartitionSpec as P

MESH = pl.DeviceIdType.MESH
F32 = jnp.float32
BF16 = jnp.bfloat16
BS = 128
VD = 512
TB = 8
CW, CCW = 0, 1


def dot(a, b):
    return jnp.dot(a, b, preferred_element_type=F32)


def kernel(
    n, keep, scale,
    inv_ref, feat_ref, w_ref, vals_hbm, cot_ref,
    act_ref, wg_ref, ig_ref,
    panel, vals, dense, acc, ys, yr, agg, pgr, gt, part, sibp, fresh, rsr,
    wl, w1, s1, w2, wp, w3, w4, wo,
    vals_sem, ag_s, ag_r, sb_s, sb_r, so_s, so_r, y_s, y_r, g_s, g_r,
    sp_s, sp_r, rs_s, rs_r, wa_s, wa_r, wb_s, wb_r, wc_s, wc_r, wd_s, wd_r, we_s, we_r,
):
    half = n // 2
    slots = vals.shape[1] - 1
    cols = n * TB
    grp = lax.axis_index("grp")
    row = lax.axis_index("row")
    core = lax.rem(row, 2)
    q = lax.div(row, 2)
    odd = lax.rem(q, 2)
    p = (1 - odd) * lax.div(q, 2) + odd * (n - lax.div(q + 1, 2))

    def chip(offset):
        at = lax.rem(p + offset + n, n)
        back = lax.div(at, half)
        return (1 - back) * 2 * at + back * (2 * (n - at) - 1)

    def peer(chip_id):
        return (grp, chip_id * 2 + core)

    sibling = (grp, q * 2 + 1 - core)
    partner = (1 - grp, row)
    across = (1 - grp, q * 2 + 1 - core)

    def rcopy(src, dst, ss, rs, dev):
        return pltpu.make_async_remote_copy(
            src_ref=src, dst_ref=dst, send_sem=ss, recv_sem=rs,
            device_id=dev, device_id_type=MESH,
        )

    load = pltpu.make_async_copy(vals_hbm, vals.at[:, pl.ds(0, slots)], vals_sem)
    load.start()

    barrier = pltpu.get_barrier_semaphore()
    for dev in [peer(chip(o)) for o in range(1, n)] + [sibling, partner, across]:
        pl.semaphore_signal(barrier, inc=1, device_id=dev, device_id_type=MESH)
    for h in range(2):
        panel[q, core * 2 + h] = feat_ref[pl.ds(h * 256, 256), :]
    for t in range(TB):
        vals[t, slots] = jnp.zeros((BS, BS), BF16)
    pl.semaphore_wait(barrier, n - 1 + 3)

    step = {CW: 1, CCW: -1}

    def lane(d, i):
        return i % 2 if d == CW else 1 - i % 2

    def ag(d, i):
        src = panel.at[chip(-step[d] * (i // 2)), core * 2 + lane(d, i)]
        return rcopy(src, src, ag_s.at[d, i], ag_r.at[d, i], peer(chip(step[d])))

    def ag_in(d, i):
        src = panel.at[chip(-step[d] * (i // 2 + 1)), core * 2 + lane(d, i)]
        return rcopy(src, src, ag_s.at[d, i], ag_r.at[d, i], peer(chip(step[d])))

    def sib(d, i, c):
        src = panel.at[chip(-step[d] * (i // 2 + 1)), c * 2 + lane(d, i)]
        return rcopy(src, src, sb_s.at[d, i], sb_r.at[d, i], sibling)

    def sib_own(c):
        src = panel.at[q, pl.ds(c * 2, 2)]
        return rcopy(src, src, so_s, so_r, sibling)

    def where_dense(chip_id):
        return chip_id if keep else 0

    def build(chip_id):
        to = where_dense(chip_id)

        def rows(t, carry):
            for j in range(TB):
                k = inv_ref[t * cols + chip_id * TB + j]
                dense[to, pl.ds(t * BS, BS), pl.ds(j * BS, BS)] = vals[t, k]
            return carry

        lax.fori_loop(0, TB, rows, 0)

    def forward(chip_id, first=False):
        build(chip_id)
        to = where_dense(chip_id)

        def rows(m, carry):
            at = pl.ds(pl.multiple_of(m * 256, 256), 256)
            v = dot(dense[to, at, :], panel[chip_id].reshape(4 * 256, 256))
            acc[at, :] = v if first else acc[at, :] + v
            return carry

        lax.fori_loop(0, 4, rows, 0)

    for i in range(2):
        for d in (CW, CCW):
            ag(d, i).start()
    sib_own(core).start()
    load.wait()

    def arrive(i):
        for d in (CW, CCW):
            ag_in(d, i).wait_recv()
            if i + 2 < n - 1:
                ag(d, i + 2).start()
            sib(d, i, core).start()

    def sib_wait(dist, d):
        for i in (2 * dist - 2, 2 * dist - 1):
            sib(d, i, 1 - core).wait_recv()

    sib_own(1 - core).wait_recv()
    forward(q, True)
    for dist in range(1, half):
        arrive(2 * dist - 2)
        if dist > 1:
            sib_wait(dist - 1, CW)
            forward(chip(-(dist - 1)))
        arrive(2 * dist - 1)
        if dist > 1:
            sib_wait(dist - 1, CCW)
            forward(chip(dist - 1))
    for d in (CW, CCW):
        sib_wait(half - 1, d)
        forward(chip(-step[d] * (half - 1)))
    far = chip(half)
    build(far)
    arrive(n - 2)
    for d in (CW, CCW):
        sib(d, n - 2, 1 - core).wait_recv()

    at_far = where_dense(far)
    mine, theirs = grp * VD, (1 - grp) * VD

    def yc(k):
        return rcopy(ys.at[k], yr.at[k], y_s.at[k], y_r.at[k], partner)

    for k in range(4):
        at = pl.ds(pl.multiple_of(theirs + k * BS, BS), BS)
        v = acc[at, :] + dot(dense[at_far, at, :], panel[far].reshape(4 * 256, 256))
        ys[k] = v.astype(BF16)
        yc(k).start()
    for k in range(2):
        at = pl.ds(pl.multiple_of(mine + k * 256, 256), 256)
        acc[at, :] += dot(dense[at_far, at, :], panel[far].reshape(4 * 256, 256))

    def gc(k, base):
        ref = gt.at[:, pl.ds(pl.multiple_of(base + k * BS, BS), BS)]
        return rcopy(ref, ref, g_s.at[k], g_r.at[k], partner)

    for k in range(4):
        yc(k).wait_recv()
        here = pl.ds(k * BS, BS)
        at = pl.ds(pl.multiple_of(mine + k * BS, BS), BS)
        a = (acc[at, :] + yr[k].astype(F32)).astype(BF16)
        agg[here, :] = a
        pre = dot(a, w_ref[...])
        s = jax.nn.sigmoid(pre)
        act_ref[here, :] = (pre * s).astype(BF16)
        grad = (cot_ref[here, :].astype(F32) * (s * (1.0 + pre * (1.0 - s)))).astype(BF16)
        pgr[here, :] = grad
        back = lax.dot_general(
            w_ref[...], grad, (((1,), (1,)), ((), ())), preferred_element_type=F32
        )
        gt[:, at] = back.astype(BF16)
        gc(k, mine).start()
    local = lax.dot_general(
        agg[...], pgr[...], (((0,), (0,)), ((), ())), preferred_element_type=F32
    )
    for c in range(2):
        wl[c] = local[c * 128 : (c + 1) * 128]

    wa = lambda: rcopy(wl.at[1 - core], w1, wa_s, wa_r, sibling)
    wb = lambda: rcopy(s1.at[1 - grp], w2, wb_s, wb_r, partner)
    wc = lambda o: rcopy(wp.at[chip(o)], w3.at[q], wc_s.at[o], wc_r.at[o], peer(chip(o)))
    wd = lambda o: rcopy(w4.at[q], w4.at[q], wd_s.at[o], wd_r.at[o], peer(chip(o)))
    me_wo = core * 2 + grp
    outs = (sibling, partner, across)
    theirs_wo = ((1 - core) * 2 + grp, core * 2 + 1 - grp, (1 - core) * 2 + 1 - grp)
    we = lambda k: rcopy(wo.at[me_wo], wo.at[me_wo], we_s.at[k], we_r.at[k], outs[k])
    share = 64 // n

    def w_stage1():
        wa().wait_recv()
        total = wl[core] + w1[...]
        for k in range(2):
            s1[k] = total[k * 64 : (k + 1) * 64]
        wb().start()

    def w_stage2():
        wb().wait_recv()
        total = s1[grp] + w2[...]
        for k in range(n):
            wp[k] = total[k * share : (k + 1) * share]
        for o in range(1, n):
            wc(o).start()
        w3[q] = wp[q]

    def w_stage3():
        for o in range(1, n):
            rcopy(wp.at[q], w3.at[chip(-o)], wc_s.at[o], wc_r.at[o], peer(chip(o))).wait_recv()
        total = w3[0]
        for k in range(1, n):
            total = total + w3[k]
        w4[q] = total * scale
        for o in range(1, n):
            wd(o).start()

    def w_stage4():
        for o in range(1, n):
            there = w4.at[chip(-o)]
            rcopy(there, there, wd_s.at[o], wd_r.at[o], peer(chip(o))).wait_recv()
        for k in range(n):
            wo[me_wo, pl.ds(k * share, share), :] = w4[k]
        for k in range(3):
            we(k).start()

    def w_stage5():
        for k in range(3):
            there = wo.at[theirs_wo[k]]
            rcopy(there, there, we_s.at[k], we_r.at[k], outs[k]).wait_recv()
        for k in range(4):
            wg_ref[pl.ds(k * 64, 64), :] = wo[k]

    wa().start()
    for k in range(4):
        gc(k, theirs).wait_recv()

    def backward(chip_id):
        if not keep:
            build(chip_id)
        to = where_dense(chip_id)
        for j in range(4):
            v = dot(gt[...], dense[to, :, pl.ds(j * 256, 256)])
            part[chip_id, j] = v.astype(BF16)
        sp(chip_id).start()

    def sp(chip_id):
        return rcopy(
            part.at[chip_id, pl.ds((1 - core) * 2, 2)], sibp.at[chip_id],
            sp_s.at[chip_id], sp_r.at[chip_id], sibling,
        )

    def rs(d, i):
        src = rsr.at[d, i + 2] if i + 2 < n - 1 else fresh.at[d, i - (n - 3)]
        return rcopy(src, rsr.at[d, i], rs_s.at[d, i], rs_r.at[d, i], peer(chip(-step[d])))

    def summed(d, i):
        chip_id = chip(-step[d] * (i // 2 + 1))
        h = lane(d, i)
        own = part[chip_id, core * 2 + h].astype(F32) + sibp[chip_id, h].astype(F32)
        if i + 2 < n - 1:
            rs(d, i + 2).wait_recv()
            rsr[d, i + 2] = (own + rsr[d, i + 2].astype(F32)).astype(BF16)
        else:
            fresh[d, i - (n - 3)] = own.astype(BF16)
        rs(d, i).start()

    backward(far)
    backward(chip(-(half - 1)))
    sp(far).wait_recv()
    for d in (CW, CCW):
        summed(d, n - 2)
    w_stage1()
    backward(chip(half - 1))
    stages = [w_stage2, w_stage3, w_stage4]
    for dist in range(half - 1, 0, -1):
        for d in (CW, CCW):
            sp(chip(-step[d] * dist)).wait_recv()
            summed(d, 2 * dist - 1)
        if dist > 1:
            backward(chip(-(dist - 1)))
            backward(chip(dist - 1))
        else:
            backward(q)
        if stages:
            stages.pop(0)()
        for d in (CW, CCW):
            summed(d, 2 * dist - 2)
    for stage in stages:
        stage()
    sp(q).wait_recv()
    for h in range(2):
        total = part[q, core * 2 + h].astype(F32) + sibp[q, h].astype(F32)
        for d in (CW, CCW):
            i = h if d == CW else 1 - h
            rs(d, i).wait_recv()
            total = total + rsr[d, i].astype(F32)
        ig_ref[pl.ds(h * 256, 256), :] = total.T.astype(BF16)
    w_stage5()

    for d in (CW, CCW):
        for i in range(n - 1):
            ag(d, i).wait_send()
            sib(d, i, core).wait_send()
            rs(d, i).wait_send()
    sib_own(core).wait_send()
    for k in range(4):
        yc(k).wait_send()
        gc(k, mine).wait_send()
    for k in range(n):
        sp(k).wait_send()
    wa().wait_send()
    wb().wait_send()
    for o in range(1, n):
        wc(o).wait_send()
        wd(o).wait_send()
    for k in range(3):
        we(k).wait_send()


def body(features, weight, block_vals, block_cols, block_count, cotangent):
    rows_dev, width = features.shape
    slots = block_vals.shape[2]
    groups = lax.axis_size("grp")
    members = lax.axis_size("row")
    verts = rows_dev * groups * members
    n = members // 2
    cols = members * rows_dev // BS
    keep = n <= 8
    live = jnp.arange(slots)[None, :] < block_count[0][:, None]
    hit = (block_cols[0][:, :, None] == jnp.arange(cols)[None, None, :]) & live[:, :, None]
    inv = slots + jnp.sum(
        jnp.where(hit, jnp.arange(slots)[None, :, None] - slots, 0), axis=1
    ).astype(jnp.int32)
    dma, vm = pltpu.SemaphoreType.DMA, pltpu.VMEM
    share = 64 // n
    scratch = [
        vm((n, 4, 256, width), BF16),
        vm((TB, slots + 1, BS, BS), BF16),
        vm((n if keep else 1, 1024, 1024), BF16),
        vm((1024, width), F32),
        vm((4, BS, width), BF16),
        vm((4, BS, width), BF16),
        vm((rows_dev, width), BF16),
        vm((rows_dev, width), BF16),
        vm((width, 1024), BF16),
        vm((n, 4, width, 256), BF16),
        vm((n, 2, width, 256), BF16),
        vm((2, 2, width, 256), BF16),
        vm((2, n - 1, width, 256), BF16),
        vm((2, 128, width), F32),
        vm((128, width), F32),
        vm((2, 64, width), F32),
        vm((64, width), F32),
        vm((n, share, width), F32),
        vm((n, share, width), F32),
        vm((n, share, width), F32),
        vm((4, 64, width), F32),
        dma,
        dma((2, n - 1)), dma((2, n - 1)),
        dma((2, n - 1)), dma((2, n - 1)),
        dma, dma,
        dma((4,)), dma((4,)), dma((4,)), dma((4,)),
        dma((n,)), dma((n,)),
        dma((2, n - 1)), dma((2, n - 1)),
        dma, dma, dma, dma,
        dma((n,)), dma((n,)), dma((n,)), dma((n,)),
        dma((3,)), dma((3,)),
    ]
    whole = pl.BlockSpec(memory_space=pltpu.VMEM)
    return pl.pallas_call(
        functools.partial(kernel, n, keep, 1.0 / math.sqrt(verts)),
        out_shape=(
            jax.ShapeDtypeStruct((rows_dev, width), BF16),
            jax.ShapeDtypeStruct((width, width), F32),
            jax.ShapeDtypeStruct((rows_dev, width), BF16),
        ),
        in_specs=[
            pl.BlockSpec(memory_space=pltpu.SMEM),
            whole,
            whole,
            pl.BlockSpec(memory_space=pl.ANY),
            whole,
        ],
        out_specs=(whole, whole, whole),
        scratch_shapes=scratch,
        compiler_params=pltpu.CompilerParams(
            collective_id=0, has_side_effects=True, vmem_limit_bytes=60 * 1024 * 1024
        ),
    )(inv.reshape(-1), features, weight, block_vals[0], cotangent)


def solution(mesh):
    placed = (
        P(("grp", "row"), None),
        P(),
        P("grp", "row", None, None, None),
        P("grp", "row", None),
        P("grp", "row"),
        P(("grp", "row"), None),
    )
    return jax.shard_map(
        body,
        mesh=mesh,
        in_specs=placed,
        out_specs=(P(("grp", "row"), None), P(), P(("grp", "row"), None)),
        check_vma=False,
    )
```

time: 387 us -> 84.2 us (0.22)
  waiting for transfers between devices: 197 us -> 0 us
  Pallas kernels: 0 us -> 76.1 us
  other arithmetic: 62.7 us -> 1.54 us
  blocking collectives: 39.9 us -> 0 us
  local copies, waits for them, and re-layouts: 44.1 us -> 5.66 us
  matrix products: 26.5 us -> 0 us
  between operations: 13.8 us -> 0.66 us
    reduce_scatter x1 -> x0, waiting for transfers between devices: 106 us -> none  [body(): lax.psum_scatter(term, 'row', scatter_dimension=0, tiled=True)]
    pallas_call x0 -> x1, Pallas kernels: none -> 76.1 us  [body(): pl.pallas_call(functools.partial(kernel, n, keep, 1.0 / math.sqrt(verts))...]
    psum x1 -> x0, waiting for transfers between devices: 51.6 us -> none  [body(): lax.psum(local_grad, ('grp', 'row')) * (1.0 / math.sqrt(verts))]
    all_gather x1 -> x0, waiting for transfers between devices: 39 us -> none  [body(): gathered = lax.all_gather(features, 'row', axis=0, tiled=True)]
    scatter-add x8 -> x0, other arithmetic: 36.9 us -> none  [spread(): return (carry.at[columns].add(contrib), None)]
    psum x1 -> x0, blocking collectives: 29.9 us -> none  [body(): summed = lax.psum(partial_value, 'grp')]
    dot_general x19 -> x0, matrix products: 26.5 us -> none  [the longest x8 12.1 us: spread(): jnp.einsum('kij,if->kjf', masked, grad_block, preferred_element_type=jnp....]
    gather x8 -> x0, local copies, waits for them, and re-layouts: 22.4 us -> none  [aggregate(): picked = panel_blocks[columns]]
  transfers between devices with their start and end apart: 3 -> 0, of which waited for: 3 -> 0; matrix products, arithmetic and copies ran while one was open for 20% -> 0% of each run, Pallas kernels for 0% -> 0%
where the time goes in v1:
time: 84.2 us; the launch traced here: 83.9 us
  Pallas kernels  76.1 us (90%)
  local copies, waits for them, and re-layouts  5.66 us (7%)
  other arithmetic  1.54 us (2%)
    pallas_call x1, Pallas kernels, body(): pl.pallas_call(functools.partial(kernel, n, keep, 1.0 / math.sqrt(verts))...  76.1 us
    unnamed x3, local copies, waits for them, and re-layouts  5.01 us

profile of v1, /device:TPU:0, one launch (start us, length us, event | category | flops | bytes accessed | tf_op | source)
XLA Modules:
  0.0 83.9 jit_solution(15577876270564492364)
XLA Ops:
  0.6 0.7 iota_compare_fusion.1
  1.4 0.8 select_reduce_fusion
  2.2 0.7 add.18.inv_ref
  2.8 76.1 %shard_map.85 = (bf16[512,256]{1,0:T(8,128)(2,1)}, f32[256,256]{1,0:T(8,128)}, bf16[512,256]{1,0:T(8,128)(2,1)}) custom-call(s32[512]{0:T(512)} %add.18.inv_ref, bf16[512,256]{1,0:T(8,128)(2,1)} %feat_ref.1, bf16[256,256]{1,0:T(8,128)(2,1)} %w_ref.1, bf16[8,16,128,128]{3,2,1,0:T(8,128)(2,1)} %bitcast.3, bf16[512,256]{1,0:T(8,128)(2,1)} %cot_ref.1), custom_call_target="tpu_custom_call" | custom-call | tf_op jit(solution)/shard_map/pallas_call | solution.py:387
  78.9 1.7 %copy.12 = bf16[512,256]{1,0:T(8,128)(2,1)} copy(bf16[512,256]{1,0:T(8,128)(2,1)} %get-tuple-element.6) | data formatting | bytes 524288
  80.6 1.7 %copy.13 = f32[256,256]{1,0:T(8,128)} copy(f32[256,256]{1,0:T(8,128)} %get-tuple-element.7) | data formatting | bytes 524288
  82.3 1.7 %copy.14 = bf16[512,256]{1,0:T(8,128)(2,1)} copy(bf16[512,256]{1,0:T(8,128)(2,1)} %get-tuple-element.8) | data formatting | bytes 524288
  (2 shorter events, 0.0 us)

commit v2 on v1

--- a/solution.py
+++ b/solution.py
@@ -23,11 +23,11 @@
 
 def kernel(
     n, keep, scale,
-    inv_ref, feat_ref, w_ref, vals_hbm, cot_ref,
+    cols_ref, count_ref, feat_ref, w_ref, vals_hbm, cot_ref,
     act_ref, wg_ref, ig_ref,
     panel, vals, dense, acc, ys, yr, agg, pgr, gt, part, sibp, fresh, rsr,
-    wl, w1, s1, w2, wp, w3, w4, wo,
-    vals_sem, ag_s, ag_r, sb_s, sb_r, so_s, so_r, y_s, y_r, g_s, g_r,
+    inv_v, inv_ref, wl, w1, s1, w2, wp, w3, w4, wo,
+    vals_sem, inv_sem, ag_s, ag_r, sb_s, sb_r, so_s, so_r, y_s, y_r, g_s, g_r,
     sp_s, sp_r, rs_s, rs_r, wa_s, wa_r, wb_s, wb_r, wc_s, wc_r, wd_s, wd_r, we_s, we_r,
 ):
     half = n // 2
@@ -62,13 +62,25 @@
     load.start()
 
     barrier = pltpu.get_barrier_semaphore()
-    for dev in [peer(chip(o)) for o in range(1, n)] + [sibling, partner, across]:
+    for dev in (peer(chip(1)), peer(chip(-1)), sibling, partner):
         pl.semaphore_signal(barrier, inc=1, device_id=dev, device_id_type=MESH)
     for h in range(2):
         panel[q, core * 2 + h] = feat_ref[pl.ds(h * 256, 256), :]
     for t in range(TB):
         vals[t, slots] = jnp.zeros((BS, BS), BF16)
-    pl.semaphore_wait(barrier, n - 1 + 3)
+    at_col = lax.broadcasted_iota(jnp.int32, (TB, cols), 1)
+    at_row = lax.broadcasted_iota(jnp.int32, (TB, cols), 0)
+    live = jnp.zeros((TB, cols), jnp.int32)
+    for t in range(TB):
+        live = jnp.where(at_row == t, count_ref[0, t], live)
+    table = jnp.full((TB, cols), slots, jnp.int32)
+    for k in range(slots):
+        hit = (cols_ref[0, :, k : k + 1] == at_col) & (live > k)
+        table = jnp.where(hit, k, table)
+    inv_v[...] = table
+    inv_copy = pltpu.make_async_copy(inv_v, inv_ref, inv_sem)
+    inv_copy.start()
+    pl.semaphore_wait(barrier, 4)
 
     step = {CW: 1, CCW: -1}
 
@@ -99,7 +111,7 @@
 
         def rows(t, carry):
             for j in range(TB):
-                k = inv_ref[t * cols + chip_id * TB + j]
+                k = inv_ref[t, chip_id * TB + j]
                 dense[to, pl.ds(t * BS, BS), pl.ds(j * BS, BS)] = vals[t, k]
             return carry
 
@@ -121,6 +133,7 @@
         for d in (CW, CCW):
             ag(d, i).start()
     sib_own(core).start()
+    inv_copy.wait()
     load.wait()
 
     def arrive(i):
@@ -334,6 +347,12 @@
         we(k).wait_send()
 
 
+def hand_vm(a, b, c, x, y, z):
+    x[...] = a[...]
+    y[...] = b[...]
+    z[...] = c[...]
+
+
 def body(features, weight, block_vals, block_cols, block_count, cotangent):
     rows_dev, width = features.shape
     slots = block_vals.shape[2]
@@ -343,11 +362,6 @@
     n = members // 2
     cols = members * rows_dev // BS
     keep = n <= 8
-    live = jnp.arange(slots)[None, :] < block_count[0][:, None]
-    hit = (block_cols[0][:, :, None] == jnp.arange(cols)[None, None, :]) & live[:, :, None]
-    inv = slots + jnp.sum(
-        jnp.where(hit, jnp.arange(slots)[None, :, None] - slots, 0), axis=1
-    ).astype(jnp.int32)
     dma, vm = pltpu.SemaphoreType.DMA, pltpu.VMEM
     share = 64 // n
     scratch = [
@@ -364,6 +378,8 @@
         vm((n, 2, width, 256), BF16),
         vm((2, 2, width, 256), BF16),
         vm((2, n - 1, width, 256), BF16),
+        vm((TB, cols), jnp.int32),
+        pltpu.SMEM((TB, cols), jnp.int32),
         vm((2, 128, width), F32),
         vm((128, width), F32),
         vm((2, 64, width), F32),
@@ -372,7 +388,7 @@
         vm((n, share, width), F32),
         vm((n, share, width), F32),
         vm((4, 64, width), F32),
-        dma,
+        dma, dma,
         dma((2, n - 1)), dma((2, n - 1)),
         dma((2, n - 1)), dma((2, n - 1)),
         dma, dma,
@@ -384,7 +400,7 @@
         dma((3,)), dma((3,)),
     ]
     whole = pl.BlockSpec(memory_space=pltpu.VMEM)
-    return pl.pallas_call(
+    results = pl.pallas_call(
         functools.partial(kernel, n, keep, 1.0 / math.sqrt(verts)),
         out_shape=(
             jax.ShapeDtypeStruct((rows_dev, width), BF16),
@@ -392,6 +408,7 @@
             jax.ShapeDtypeStruct((rows_dev, width), BF16),
         ),
         in_specs=[
+            whole,
             pl.BlockSpec(memory_space=pltpu.SMEM),
             whole,
             whole,
@@ -403,7 +420,11 @@
         compiler_params=pltpu.CompilerParams(
             collective_id=0, has_side_effects=True, vmem_limit_bytes=60 * 1024 * 1024
         ),
-    )(inv.reshape(-1), features, weight, block_vals[0], cotangent)
+    )(block_cols, block_count, features, weight, block_vals[0], cotangent)
+    return pl.pallas_call(
+        hand_vm,
+        out_shape=tuple(jax.ShapeDtypeStruct(r.shape, r.dtype) for r in results),
+    )(*results)
 
 
 def solution(mesh):

time: 84.2 us -> 76.4 us (0.907)
  local copies, waits for them, and re-layouts: 5.66 us -> 0 us
  other arithmetic: 1.54 us -> 0 us
    unnamed x3 -> x0, local copies, waits for them, and re-layouts: 5.01 us -> none
    pallas_call x1, Pallas kernels: 76.1 us -> 73.6 us  [body(): pl.pallas_call(functools.partial(kernel, n, keep, 1.0 / math.sqrt(verts))...]
    pallas_call x0 -> x1, Pallas kernels: none -> 2 us  [body(): pl.pallas_call(hand_vm, out_shape=tuple((jax.ShapeDtypeStruct(r.shape, r....]
where the time goes in v2:
time: 76.4 us; the launch traced here: 76.2 us
  Pallas kernels  75.6 us (99%)
    pallas_call x1, Pallas kernels, body(): pl.pallas_call(functools.partial(kernel, n, keep, 1.0 / math.sqrt(verts))...  73.6 us
    pallas_call x1, Pallas kernels, body(): pl.pallas_call(hand_vm, out_shape=tuple((jax.ShapeDtypeStruct(r.shape, r....  2 us

profile of v2, /device:TPU:0, one launch (start us, length us, event | category | flops | bytes accessed | tf_op | source)
XLA Modules:
  0.0 76.2 jit_solution(7712463343416507208)
XLA Ops:
  0.6 73.6 %shard_map.85 = (bf16[512,256]{1,0:T(8,128)(2,1)}, f32[256,256]{1,0:T(8,128)}, bf16[512,256]{1,0:T(8,128)(2,1)}) custom-call(s32[1,8,16]{2,1,0:T(8,128)} %cols_ref.1, s32[1,8]{1,0:T(1,128)} %count_ref.1, bf16[512,256]{1,0:T(8,128)(2,1)} %feat_ref.1, bf16[256,256]{1,0:T(8,128)(2,1)} %w_ref.1, bf16[8,16,128,128]{3,2,1,0:T(8,128)(2,1)} %bitcast.1, ...), custom_call_target="tpu_custom_call" | custom-call | tf_op jit(solution)/shard_map/pallas_call | solution.py:403
  74.2 2.0 %shard_map.86 = (bf16[512,256]{1,0:T(8,128)(2,1)}, f32[256,256]{1,0:T(8,128)}, bf16[512,256]{1,0:T(8,128)(2,1)}) custom-call(bf16[512,256]{1,0:T(8,128)(2,1)} %get-tuple-element.6.a, f32[256,256]{1,0:T(8,128)} %get-tuple-element.7.b, bf16[512,256]{1,0:T(8,128)(2,1)} %get-tuple-element.8.c), custom_call_target="tpu_custom_call" | custom-call | tf_op jit(solution)/shard_map/pallas_call | solution.py:424
